TPU v7x, 32 devices: a whole 2x2x4 slice. The times are simulated.
32 devices in a mesh: ta: 4 (over z), xyz: 8 (over y, x, core).
Axes of the slice: x: 2, y: 2, z: 4, core: 2. Of those that a mesh axis runs over, the one named last changes fastest.
Arguments:
- residual: bfloat16 [512, 4608], P(('ta', 'xyz')), may hold values from -6 to 6
- iterate: bfloat16 [512, 4608], P(('ta', 'xyz')), may hold values from -6 to 6
- prolongator: bfloat16 [512, 12288], P(('ta', 'xyz')), may hold values from -0.3125 to 0.3125
- coarse_links: bfloat16 [9, 1024, 2048], P(None, ('ta', 'xyz')), may hold values from -0.125 to 0.125
- owner_counts: int32 [4, 8], P('ta'), may hold values from 1 to 32, 128 in all within a row
Outputs:
- corrected: bfloat16 [512, 4608], P(('ta', 'xyz'))
Inputs may be any that keep to these rules, and one draw needn't show every extreme that they name: `owner_counts`: row t gives how many sites of time slice t each xyz index owns; each row sums to 128 and its largest entry is exactly 32.
All inputs are finite; a program needn't handle non-finite values.
Results may differ from a plain program's by a relative error of at most 0.0038.
Values may be sent and summed in bfloat16 or wider, within the bound.
A program may use at most 64 MiB of HBM per device.

v0:
```python
import jax
import jax.numpy as jnp
from jax import lax
from jax.sharding import PartitionSpec as P

NV = 32
FB = 192
RHS = 12
LY = 2
LZ = 8
SWEEPS = 2


def with_halo(block, sides, width):
    for axis, dim in sides:
        count = lax.axis_size(axis)
        forward = [(i, i + 1) for i in range(count - 1)]
        forward.append((count - 1, 0))
        backward = [(target, source) for source, target in forward]
        low = lax.ppermute(
            lax.slice_in_dim(block, block.shape[dim] - width, None, axis=dim), axis, forward
        )
        high = lax.ppermute(lax.slice_in_dim(block, 0, width, axis=dim), axis, backward)
        block = jnp.concatenate([low, block, high], axis=dim)
    return block


def basis_block(basis_rows):
    count_rows = basis_rows.shape[0]
    matrix = basis_rows.reshape(count_rows, 2, NV, FB)
    real_rows = jnp.concatenate([matrix[:, 0], matrix[:, 1]], axis=2)
    imag_rows = jnp.concatenate([-matrix[:, 1], matrix[:, 0]], axis=2)
    return jnp.concatenate([real_rows, imag_rows], axis=1)


def restrict(fine_rows, block):
    count_rows = fine_rows.shape[0]
    vector = fine_rows.reshape(count_rows, RHS, 2 * FB)
    result = jnp.einsum("bkf,brf->brk", block, vector, preferred_element_type=jnp.float32)
    return result.reshape(count_rows, RHS * 2 * NV).astype(jnp.bfloat16)


def prolong(coarse_rows, block):
    count_rows = coarse_rows.shape[0]
    vector = coarse_rows.reshape(count_rows, RHS, 2 * NV)
    result = jnp.einsum("bkf,brk->brf", block, vector, preferred_element_type=jnp.float32)
    return result.reshape(count_rows, RHS * 2 * FB)


def link_block(link_rows):
    count_rows = link_rows.shape[1]
    matrix = link_rows.reshape(9, count_rows, 2, NV, NV)
    real_rows = jnp.concatenate([matrix[:, :, 0], -matrix[:, :, 1]], axis=3)
    imag_rows = jnp.concatenate([matrix[:, :, 1], matrix[:, :, 0]], axis=3)
    return jnp.concatenate([real_rows, imag_rows], axis=2)


def hopping(link_real, neighbours):
    count_rows = neighbours.shape[1]
    vector = neighbours.reshape(9, count_rows, RHS, 2 * NV)
    result = jnp.einsum("mskj,msrj->srk", link_real, vector, preferred_element_type=jnp.float32)
    return result.reshape(count_rows, RHS * 2 * NV)


def spatial_neighbours(positions, slab_rows):
    extent_x = slab_rows // (LY * LZ)
    coord_x = positions % extent_x
    coord_z = positions // extent_x % LZ
    coord_y = positions // (extent_x * LZ)

    def site_of(along_x, along_y, along_z):
        return (along_y % LY * LZ + along_z % LZ) * extent_x + along_x % extent_x

    return [
        site_of(coord_x + 1, coord_y, coord_z),
        site_of(coord_x - 1, coord_y, coord_z),
        site_of(coord_x, coord_y + 1, coord_z),
        site_of(coord_x, coord_y - 1, coord_z),
        site_of(coord_x, coord_y, coord_z + 1),
        site_of(coord_x, coord_y, coord_z - 1),
    ]


def tile_source(positions, run_starts, run_ends, capacity):
    owners = jnp.sum((run_ends[None, :] <= positions[:, None]).astype(jnp.int32), axis=1)
    ranks = jnp.arange(run_ends.shape[0], dtype=jnp.int32)
    begin = jnp.sum(jnp.where(ranks[None, :] == owners[:, None], run_starts[None, :], 0), axis=1)
    return owners * capacity + positions - begin


def owned_positions(counts_row, owner_index, slots, slab_rows):
    run_starts = jnp.cumsum(counts_row) - counts_row
    return jnp.minimum(run_starts[owner_index] + slots, slab_rows - 1)


def whole_rims(slice_rows):
    return with_halo(slice_rows[None], (("ta", 0),), 1)


def on_device(residual, iterate, prolongator, coarse_links, owner_counts):
    owner_index = lax.axis_index("xyz")
    block_count = residual.shape[0]
    capacity = coarse_links.shape[1]
    counts_row = owner_counts[0]
    run_ends = jnp.cumsum(counts_row)
    run_starts = run_ends - counts_row
    basis_real = basis_block(prolongator)
    link_real = link_block(coarse_links)
    coarse_rhs = restrict(residual, basis_real)
    slice_rows = lax.all_gather(coarse_rhs, "xyz", axis=0, tiled=True)
    slab_rows = slice_rows.shape[0]
    slots = jnp.arange(capacity, dtype=jnp.int32)
    positions = owned_positions(counts_row, owner_index, slots, slab_rows)
    occupied = slots < counts_row[owner_index]
    spatial_rows = spatial_neighbours(positions, slab_rows)
    owned_rhs = jnp.take(slice_rows, positions, axis=0).astype(jnp.float32)
    source = tile_source(jnp.arange(slab_rows, dtype=jnp.int32), run_starts, run_ends, capacity)
    own_piece = coarse_rhs
    for sweep_index in range(SWEEPS):
        surround = whole_rims(slice_rows)
        here_rows = surround[1]
        after_rows = jnp.take(surround[2], positions, axis=0)
        before_rows = jnp.take(surround[0], positions, axis=0)
        row_list = [jnp.take(here_rows, positions, axis=0)]
        row_list = row_list + [jnp.take(here_rows, rows, axis=0) for rows in spatial_rows]
        row_list = row_list + [after_rows, before_rows]
        neighbours = jnp.stack(row_list)
        updated = owned_rhs - hopping(link_real, neighbours)
        owned_tile = jnp.where(occupied[:, None], updated, 0.0).astype(jnp.bfloat16)
        slice_rows = jnp.take(lax.all_gather(owned_tile, "xyz", axis=0, tiled=True), source, axis=0)
        own_piece = lax.dynamic_slice_in_dim(slice_rows, owner_index * block_count, block_count, 0)
    correction = prolong(own_piece, basis_real)
    return (iterate.astype(jnp.float32) + correction).astype(jnp.bfloat16)


def solution(mesh):
    in_specs = (
        P(("ta", "xyz"), None),
        P(("ta", "xyz"), None),
        P(("ta", "xyz"), None),
        P(None, ("ta", "xyz"), None),
        P("ta", None),
    )
    out_specs = P(("ta", "xyz"), None)
    return jax.shard_map(
        on_device, mesh=mesh, in_specs=in_specs, out_specs=out_specs, check_vma=False
    )
```

profile of v0, /device:TPU:0, one launch (start us, length us, event | category | flops | bytes accessed | tf_op | source)
XLA Modules:
  0.0 114.6 jit_solution(2540627490024351829)
XLA Ops:
  0.0 1.7 %reshape.90 = bf16[16,2,32,192]{3,2,1,0:T(8,128)(2,1)S(1)} reshape(bf16[16,12288]{1,0:T(8,128)(2,1)} %param.11) | data formatting | bytes 786432 | tf_op jit(solution)/shard_map/reshape | solution.py:30
  2.8 10.7 %all_gather.9 = bf16[128,768]{1,0:T(8,128)(2,1)S(1)} all-gather(bf16[16,768]{1,0:T(8,128)(2,1)S(1)} %convert_element_type.30), channel_id=1, replica_groups=mesh['ta'=4,'xyz'=8] {'xyz'}, dimensions={0}, use_global_device_ids=true | all-gather | bytes 221184 | tf_op jit(solution)/shard_map/all_gather | solution.py:110
  13.5 3.6 %collective-permute-start = (bf16[1,128,768]{2,1,0:T(8,128)(2,1)S(1)}, bf16[1,128,768]{2,1,0:T(8,128)(2,1)S(1)}, u32[]{:S(2)}, u32[]{:S(2)}) collective-permute-start(bf16[1,128,768]{2,1,0:T(8,128)(2,1)S(1)} %bitcast.86), channel_id=1, source_target_pairs={{8,0},{16,8},{24,16},{0,24},{9,1},{17,9},{25,17},{1,25},{10,2},{18... | collective-permute-start | bytes 589832 | tf_op jit(solution)/shard_map/ppermute | solution.py:23
  29.0 0.8 stack.65
  31.3 4.8 %reshape.94 = bf16[9,32,2,32,32]{4,3,2,1,0:T(8,128)(2,1)} reshape(bf16[9,32,2048]{2,1,0:T(8,128)(2,1)S(1)} %copy-done) | data formatting | bytes 2359296 | tf_op jit(solution)/shard_map/reshape | solution.py:52
  36.1 3.5 %fusion.30 = (bf16[9,32,1,32,32]{4,3,2,1,0:T(8,128)(2,1)S(1)}, bf16[9,32,1,32,32]{4,3,2,1,0:T(8,128)(2,1)S(1)}) fusion(bf16[9,32,2,32,32]{4,3,2,1,0:T(8,128)(2,1)} %reshape.94), kind=kLoop, calls=%fused_computation.173 | loop fusion | bytes 2359296 | tf_op jit(solution)/shard_map/slice | solution.py:53
  40.0 3.0 %copy_bitcast_fusion = (bf16[9,32,32,32]{3,2,0,1:T(8,128)(2,1)}, bf16[9,32,32,32]{3,2,0,1:T(8,128)(2,1)}) fusion(bf16[9,32,1,32,32]{4,3,2,1,0:T(8,128)(2,1)S(1)} %get-tuple-element.9, bf16[9,32,1,32,32]{4,3,2,1,0:T(8,128)(2,1)S(1)} %get-tuple-element.10), kind=kLoop, calls=%fused_computation.21 | loop fusion | bytes 2359296 | tf_op jit(solution)/shard_map/squeeze | solution.py:53
  44.4 1.3 %gather_fusion.7 = bf16[32,768]{1,0:T(8,128)(2,1)} fusion(bf16[128,768]{1,0:T(8,128)(2,1)S(1)} %bitcast.90, s32[1024]{0:T(1024)S(1)} %pad_clamp_fusion.7), kind=kCustom, calls=%fused_computation.8.clone | custom fusion | bytes 98432 | tf_op jit(solution)/shard_map/jit(_take)/gather | solution.py:122
  45.7 1.3 %gather_fusion.8 = bf16[32,768]{1,0:T(8,128)(2,1)} fusion(bf16[128,768]{1,0:T(8,128)(2,1)S(1)} %bitcast.89, s32[1024]{0:T(1024)S(1)} %pad_clamp_fusion.7), kind=kCustom, calls=%fused_computation.9.clone | custom fusion | bytes 98432 | tf_op jit(solution)/shard_map/jit(_take)/gather | solution.py:123
  47.0 0.9 broadcast_select_fusion.15
  48.9 0.8 stack.68
  55.3 6.1 %convolution_bitcast_fusion.1 = f32[32,12,64]{2,1,0:T(8,128)S(1)} fusion(bf16[9,32,12,64]{3,2,0,1:T(8,128)(2,1)} %bitcast_dynamic-update-slice_fusion.9, bf16[9,32,32,32]{3,2,0,1:T(8,128)(2,1)} %get-tuple-element.32, bf16[9,32,32,32]{3,2,0,1:T(8,128)(2,1)} %get-tuple-element.31, bf16[9,32,32,32]{3,2,0,1:T(8,128)(2,1)S(1)} %fusion.29), kind=kOutput, calls=%fused_computation.24 | convolution fusion | flops 37748736 | bytes 2310144 | tf_op jit(solution)/shard_map/mskj,msrj->srk/dot_general | solution.py:61
  61.6 9.6 %all_gather.10 = bf16[256,768]{1,0:T(8,128)(2,1)S(1)} all-gather(bf16[32,768]{1,0:T(8,128)(2,1)S(1)} %fusion.3), channel_id=1, replica_groups=mesh['ta'=4,'xyz'=8] {'xyz'}, dimensions={0}, use_global_device_ids=true | all-gather | bytes 442368 | tf_op jit(solution)/shard_map/all_gather | solution.py:130
  71.1 0.9 gather_fusion.9
  72.8 3.8 %collective-permute-start.2 = (bf16[1,128,768]{2,1,0:T(8,128)(2,1)}, bf16[1,128,768]{2,1,0:T(8,128)(2,1)S(1)}, u32[]{:S(2)}, u32[]{:S(2)}) collective-permute-start(bf16[1,128,768]{2,1,0:T(8,128)(2,1)} %fusion.35), channel_id=1, source_target_pairs={{8,0},{16,8},{24,16},{0,24},{9,1},{17,9},{25,17},{1,25},{10,2},{18... | collective-permute-start | bytes 589832 | tf_op jit(solution)/shard_map/ppermute | solution.py:23
  81.3 1.4 %gather_fusion.16 = bf16[32,768]{1,0:T(8,128)(2,1)} fusion(bf16[128,768]{1,0:T(8,128)(2,1)S(1)} %broadcast_select_fusion, s32[1024]{0:T(1024)} %copy-done.20), kind=kCustom, calls=%fused_computation.16.clone | custom fusion | bytes 98432 | tf_op jit(solution)/shard_map/jit(_take)/gather | solution.py:125
  83.8 0.9 broadcast_select_fusion.1
  84.7 0.8 stack.76
  85.5 1.4 %gather_fusion.17 = bf16[32,768]{1,0:T(8,128)(2,1)} fusion(bf16[128,768]{1,0:T(8,128)(2,1)S(1)} %bitcast.92, s32[1024]{0:T(1024)} %copy-done.14), kind=kCustom, calls=%fused_computation.17.clone | custom fusion | bytes 98432 | tf_op jit(solution)/shard_map/jit(_take)/gather | solution.py:122
  86.9 1.5 %gather_fusion.18 = bf16[32,768]{1,0:T(8,128)(2,1)} fusion(bf16[128,768]{1,0:T(8,128)(2,1)S(1)} %bitcast.91, s32[1024]{0:T(1024)} %copy-done.14), kind=kCustom, calls=%fused_computation.18.clone | custom fusion | bytes 98432 | tf_op jit(solution)/shard_map/jit(_take)/gather | solution.py:123
  88.4 0.9 broadcast_select_fusion.13
  96.7 6.1 %convolution_bitcast_fusion = f32[32,12,64]{2,1,0:T(8,128)S(1)} fusion(bf16[9,32,12,64]{3,2,0,1:T(8,128)(2,1)} %bitcast_dynamic-update-slice_fusion, bf16[9,32,32,32]{3,2,0,1:T(8,128)(2,1)} %get-tuple-element.32, bf16[9,32,32,32]{3,2,0,1:T(8,128)(2,1)} %get-tuple-element.31, bf16[9,32,32,32]{3,2,0,1:T(8,128)(2,1)S(1)} %fusion.29), kind=kOutput, calls=%fused_computation.23 | convolution fusion | flops 37748736 | bytes 2310144 | tf_op jit(solution)/shard_map/mskj,msrj->srk/dot_general | solution.py:61
  103.1 8.7 %all_gather.11 = bf16[256,768]{1,0:T(8,128)(2,1)S(1)} all-gather(bf16[32,768]{1,0:T(8,128)(2,1)S(1)} %fusion.5), channel_id=1, replica_groups=mesh['ta'=4,'xyz'=8] {'xyz'}, dimensions={0}, use_global_device_ids=true | all-gather | bytes 442368 | tf_op jit(solution)/shard_map/all_gather | solution.py:130
  111.8 1.0 gather_fusion.19
  (182 shorter events, 38.6 us)
Async XLA Ops:
  1.9 15.2 %copy-start.37 = (s32[1,8]{1,0:T(1,128)S(1)}, s32[1,8]{1,0:T(1,128)}, u32[]{:S(2)}) copy-start(s32[1,8]{1,0:T(1,128)} %param.13) | copy-start | bytes 100
  13.5 30.9 %collective-permute-start = (bf16[1,128,768]{2,1,0:T(8,128)(2,1)S(1)}, bf16[1,128,768]{2,1,0:T(8,128)(2,1)S(1)}, u32[]{:S(2)}, u32[]{:S(2)}) collective-permute-start(bf16[1,128,768]{2,1,0:T(8,128)(2,1)S(1)} %bitcast.86), channel_id=1, source_target_pairs={{8,0},{16,8},{24,16},{0,24},{9,1},{17,9},{25,17},{1,25},{10,2},{18... | collective-permute-start | bytes 589832 | tf_op jit(solution)/shard_map/ppermute | solution.py:23
  17.1 28.6 %collective-permute-start.1 = (bf16[1,128,768]{2,1,0:T(8,128)(2,1)S(1)}, bf16[1,128,768]{2,1,0:T(8,128)(2,1)S(1)}, u32[]{:S(2)}, u32[]{:S(2)}) collective-permute-start(bf16[1,128,768]{2,1,0:T(8,128)(2,1)S(1)} %bitcast.87), channel_id=1, source_target_pairs={{0,8},{8,16},{16,24},{24,0},{1,9},{9,17},{17,25},{25,1},{2,10},{10... | collective-permute-start | bytes 589832 | tf_op jit(solution)/shard_map/ppermute | solution.py:20
  19.2 27.8 %copy-start.22 = (pred[32]{0:T(512)(128)(4,1)}, pred[32]{0:T(512)(128)(4,1)S(1)}, u32[]{:S(2)}) copy-start(pred[32]{0:T(512)(128)(4,1)S(1)} %compare_and_fusion.7) | copy-start | bytes 100
  20.6 7.5 %copy-start.28 = (pred[32]{0:T(512)(128)(4,1)}, pred[32]{0:T(512)(128)(4,1)S(1)}, u32[]{:S(2)}) copy-start(pred[32]{0:T(512)(128)(4,1)S(1)} %get-tuple-element.29) | copy-start | bytes 100
  20.6 7.5 %copy-start.32 = (pred[32]{0:T(512)(128)(4,1)}, pred[32]{0:T(512)(128)(4,1)S(1)}, u32[]{:S(2)}) copy-start(pred[32]{0:T(512)(128)(4,1)S(1)} %get-tuple-element.30) | copy-start | bytes 100
  21.9 6.1 %copy-start.24 = (pred[32]{0:T(512)(128)(4,1)}, pred[32]{0:T(512)(128)(4,1)S(1)}, u32[]{:S(2)}) copy-start(pred[32]{0:T(512)(128)(4,1)S(1)} %get-tuple-element.27) | copy-start | bytes 100
  21.9 6.1 %copy-start.30 = (pred[32]{0:T(512)(128)(4,1)}, pred[32]{0:T(512)(128)(4,1)S(1)}, u32[]{:S(2)}) copy-start(pred[32]{0:T(512)(128)(4,1)S(1)} %get-tuple-element.28) | copy-start | bytes 100
  23.3 7.1 %copy-start.23 = (pred[32]{0:T(512)(128)(4,1)}, pred[32]{0:T(512)(128)(4,1)S(1)}, u32[]{:S(2)}) copy-start(pred[32]{0:T(512)(128)(4,1)S(1)} %get-tuple-element.25) | copy-start | bytes 100
  24.0 21.7 %copy-start.14 = (s32[1024]{0:T(1024)}, s32[1024]{0:T(1024)S(1)}, u32[]{:S(2)}) copy-start(s32[1024]{0:T(1024)S(1)} %pad_clamp_fusion.7) | copy-start | bytes 12292
  44.4 17.1 %copy-start.34 = (pred[32]{0:T(512)(128)(4,1)}, pred[32]{0:T(512)(128)(4,1)S(1)}, u32[]{:S(2)}) copy-start(pred[32]{0:T(512)(128)(4,1)S(1)} %iota_compare_fusion.2) | copy-start | bytes 100
  44.4 26.7 %copy-start.21 = (s32[1024]{0:T(1024)}, s32[1024]{0:T(1024)S(1)}, u32[]{:S(2)}) copy-start(s32[1024]{0:T(1024)S(1)} %pad_clamp_fusion) | copy-start | bytes 12292
  45.7 6.7 %copy-start.1 = (bf16[1,32,12,64]{3,2,1,0:T(8,128)(2,1)S(1)}, bf16[1,32,12,64]{3,2,1,0:T(8,128)(2,1)}, u32[]{:S(2)}) copy-start(bf16[1,32,12,64]{3,2,1,0:T(8,128)(2,1)} %stack.65) | copy-start | bytes 147460
  45.7 7.5 %copy-start.2 = (bf16[1,32,12,64]{3,2,1,0:T(8,128)(2,1)S(1)}, bf16[1,32,12,64]{3,2,1,0:T(8,128)(2,1)}, u32[]{:S(2)}) copy-start(bf16[1,32,12,64]{3,2,1,0:T(8,128)(2,1)} %stack.66) | copy-start | bytes 147460
  72.8 12.7 %collective-permute-start.2 = (bf16[1,128,768]{2,1,0:T(8,128)(2,1)}, bf16[1,128,768]{2,1,0:T(8,128)(2,1)S(1)}, u32[]{:S(2)}, u32[]{:S(2)}) collective-permute-start(bf16[1,128,768]{2,1,0:T(8,128)(2,1)} %fusion.35), channel_id=1, source_target_pairs={{8,0},{16,8},{24,16},{0,24},{9,1},{17,9},{25,17},{1,25},{10,2},{18... | collective-permute-start | bytes 589832 | tf_op jit(solution)/shard_map/ppermute | solution.py:23
  76.6 10.3 %collective-permute-start.3 = (bf16[1,128,768]{2,1,0:T(8,128)(2,1)}, bf16[1,128,768]{2,1,0:T(8,128)(2,1)S(1)}, u32[]{:S(2)}, u32[]{:S(2)}) collective-permute-start(bf16[1,128,768]{2,1,0:T(8,128)(2,1)} %fusion.35), channel_id=1, source_target_pairs={{0,8},{8,16},{16,24},{24,0},{1,9},{9,17},{17,25},{25,1},{2,10},{10... | collective-permute-start | bytes 589832 | tf_op jit(solution)/shard_map/ppermute | solution.py:20
  76.7 5.9 %copy-start.33 = (pred[32]{0:T(512)(128)(4,1)S(1)}, pred[32]{0:T(512)(128)(4,1)}, u32[]{:S(2)}) copy-start(pred[32]{0:T(512)(128)(4,1)} %copy-done.32) | copy-start | bytes 100
  77.5 5.6 %copy-start.31 = (pred[32]{0:T(512)(128)(4,1)S(1)}, pred[32]{0:T(512)(128)(4,1)}, u32[]{:S(2)}) copy-start(pred[32]{0:T(512)(128)(4,1)} %copy-done.30) | copy-start | bytes 100
  86.9 7.7 %copy-start.3 = (bf16[1,32,12,64]{3,2,1,0:T(8,128)(2,1)S(1)}, bf16[1,32,12,64]{3,2,1,0:T(8,128)(2,1)}, u32[]{:S(2)}) copy-start(bf16[1,32,12,64]{3,2,1,0:T(8,128)(2,1)} %stack.76) | copy-start | bytes 147460
  96.7 6.2 %copy-start.35 = (pred[32]{0:T(512)(128)(4,1)S(1)}, pred[32]{0:T(512)(128)(4,1)}, u32[]{:S(2)}) copy-start(pred[32]{0:T(512)(128)(4,1)} %copy-done.34) | copy-start | bytes 100
  102.8 10.0 %copy-start.36 = (pred[16]{0:T(512)(128)(4,1)S(1)}, pred[16]{0:T(512)(128)(4,1)}, u32[]{:S(2)}) copy-start(pred[16]{0:T(512)(128)(4,1)} %dynamic-slice.1) | copy-start | bytes 52
  102.8 10.2 %copy-start.7 = (bf16[16,32,192]{2,1,0:T(8,128)(2,1)S(1)}, bf16[16,32,192]{2,1,0:T(8,128)(2,1)}, u32[]{:S(2)}) copy-start(bf16[16,32,192]{2,1,0:T(8,128)(2,1)} %copy-done.6) | copy-start | bytes 589828
  102.8 10.1 %copy-start.9 = (bf16[16,32,192]{2,1,0:T(8,128)(2,1)S(1)}, bf16[16,32,192]{2,1,0:T(8,128)(2,1)}, u32[]{:S(2)}) copy-start(bf16[16,32,192]{2,1,0:T(8,128)(2,1)} %copy-done.8) | copy-start | bytes 589828
  102.9 10.1 %copy-start.11 = (bf16[16,32,192]{2,1,0:T(8,128)(2,1)S(1)}, bf16[16,32,192]{2,1,0:T(8,128)(2,1)}, u32[]{:S(2)}) copy-start(bf16[16,32,192]{2,1,0:T(8,128)(2,1)} %copy-done.10) | copy-start | bytes 589828
  (18 other events, 45.2 us)
where the time goes:
time: 115 us
  local copies, waits for them, and re-layouts  52.4 us (46%)
  blocking collectives  29 us (25%)
  matrix products  12.9 us (11%)
  other arithmetic  12.1 us (11%)
  starting transfers between devices  7.43 us (6%)
    all_gather x2, blocking collectives, on_device(): lax.all_gather(owned_tile, 'xyz', axis=0, tiled=True)  18.3 us
    unnamed x93, local copies, waits for them, and re-layouts  12.2 us
    dot_general x2, matrix products, hopping(): jnp.einsum('mskj,msrj->srk', link_real, vector, preferred_element_type=jn...  12.1 us
    all_gather x1, blocking collectives, on_device(): slice_rows = lax.all_gather(coarse_rhs, 'xyz', axis=0, tiled=True)  10.7 us
    gather x12, local copies, waits for them, and re-layouts, on_device(): jnp.take(here_rows, rows, axis=0)  8.9 us
    ppermute x2, starting transfers between devices, with_halo(): lax.ppermute(lax.slice_in_dim(block, 0, width, axis=dim), axis, backward)  7.42 us
    another operation x20, local copies, waits for them, and re-layouts, on_device(): neighbours = jnp.stack(row_list)  7.28 us
    reshape x1, local copies, waits for them, and re-layouts, link_block(): matrix = link_rows.reshape(9, count_rows, 2, NV, NV)  4.83 us
  transfers between devices with their start and end apart: 4, of which 0 were waited for; matrix products, arithmetic and copies ran while one was open for 33% of the time, Pallas kernels for 0%

commit v1 on v0

v1 whole, which is shorter than its diff:
```python
import functools

import jax
import jax.numpy as jnp
from jax import lax
from jax.experimental import pallas as pl
from jax.experimental.pallas import tpu as pltpu
from jax.sharding import PartitionSpec as P

NV = 32
FB = 192
RHS = 12
LY = 2
LZ = 8
SWEEPS = 2
COLS = RHS * 2 * NV
LANES = 128
UNITS = COLS // LANES
GROUP = 16
MESH = pl.DeviceIdType.MESH
F32 = jnp.float32
BF16 = jnp.bfloat16


def basis_block(basis_rows):
    count_rows = basis_rows.shape[0]
    matrix = basis_rows.reshape(count_rows, 2, NV, FB)
    real_rows = jnp.concatenate([matrix[:, 0], matrix[:, 1]], axis=2)
    imag_rows = jnp.concatenate([-matrix[:, 1], matrix[:, 0]], axis=2)
    return jnp.concatenate([real_rows, imag_rows], axis=1)


def restrict(fine_rows, block):
    count_rows = fine_rows.shape[0]
    vector = fine_rows.reshape(count_rows, RHS, 2 * FB)
    result = jnp.einsum("bkf,brf->brk", block, vector, preferred_element_type=F32)
    return result.reshape(count_rows, COLS).astype(BF16)


def prolong(coarse_rows, block):
    count_rows = coarse_rows.shape[0]
    vector = coarse_rows.reshape(count_rows, RHS, 2 * NV)
    result = jnp.einsum("bkf,brk->brf", block, vector, preferred_element_type=F32)
    return result.reshape(count_rows, RHS * 2 * FB)


def iota(shape, dim):
    return lax.broadcasted_iota(jnp.int32, shape, dim)


def dot(left, right):
    return jnp.dot(left, right, preferred_element_type=F32)


def dot_nt(left, right):
    return lax.dot_general(left, right, (((1,), (1,)), ((), ())), preferred_element_type=F32)


def one_hot(condition):
    return jnp.where(condition, 1.0, 0.0).astype(BF16)


def shifted_sites(site, extent_x):
    bits_x = extent_x.bit_length() - 1
    x = site & (extent_x - 1)
    z = (site >> bits_x) & (LZ - 1)
    y = site >> (bits_x + 3)

    def site_of(ax, ay, az):
        return ((((ay & (LY - 1)) << 3) + (az & (LZ - 1))) << bits_x) + (ax & (extent_x - 1))

    return [
        site,
        site_of(x - 1, y, z),
        site_of(x + 1, y, z),
        site_of(x, y - 1, z),
        site_of(x, y + 1, z),
        site_of(x, y, z - 1),
        site_of(x, y, z + 1),
    ]


def coarse_kernel(
    n_ta, n_xyz, cap, block,
    rhs_ref, counts_ref, links_hbm, own_ref,
    vec, tiles, fin, scat, zin, zout, cnt, links, weights, lhs, part, perm, pick,
    send_a, recv_a, send_c, recv_c, send_e, recv_e, send_z, recv_z, send_n, recv_n, sem_l,
):
    slab = n_xyz * block
    extent_x = slab // (LY * LZ)
    t = lax.axis_index("ta")
    o = lax.axis_index("xyz")
    up = lax.rem(t + 1, n_ta)
    down = lax.rem(t + n_ta - 1, n_ta)
    peers = [lax.rem(o + d, n_xyz) for d in range(1, n_xyz)]

    load = pltpu.make_async_copy(links_hbm, links, sem_l)
    load.start()
    barrier = pltpu.get_barrier_semaphore()
    for peer in peers:
        pl.semaphore_signal(barrier, inc=1, device_id=(t, peer), device_id_type=MESH)
    for row in (up, down):
        pl.semaphore_signal(barrier, inc=1, device_id=(row, o), device_id_type=MESH)

    cnt[0] = jnp.zeros((8, LANES), jnp.int32)
    cnt[0, 0:1, 0:n_xyz] = counts_ref[...]
    mine = pl.ds(pl.multiple_of(o * block, block), block)
    my_tile = pl.ds(pl.multiple_of(o * cap, cap), cap)
    vec[mine, :] = rhs_ref[...]
    pl.semaphore_wait(barrier, n_xyz + 1)

    def remote(src, dst, send, recv, device):
        copy = pltpu.make_async_remote_copy(
            src_ref=src, dst_ref=dst, send_sem=send, recv_sem=recv,
            device_id=device, device_id_type=MESH,
        )
        copy.start()
        return copy

    def to_slice(src_of, dst, send, recv):
        return [
            remote(src_of(peer), dst, send.at[d], recv.at[d], (t, peer))
            for d, peer in enumerate(peers)
        ]

    copies_n = [
        remote(cnt.at[0], cnt.at[1 + side], send_n.at[side], recv_n.at[side], (row, o))
        for side, row in enumerate((down, up))
    ]
    copies_a = to_slice(lambda peer: vec.at[mine], vec.at[mine], send_a, recv_a)

    r_id, c_id = iota((512, 512), 0), iota((512, 512), 1)
    perm[...] = one_hot(c_id == ((r_id >> 5) & 3) * 128 + (r_id >> 7) * 32 + (r_id & 31))
    pick[...] = one_hot((iota((2048, LANES), 0) >> 4) == iota((2048, LANES), 1))

    counts = cnt[0, 0:1, :].astype(F32)
    lane = iota((1, LANES), 1)

    def start_of(row):
        return jnp.sum(jnp.where(lane < o, row, 0.0), axis=1, keepdims=True).astype(jnp.int32)

    start = start_of(counts)
    own_count = jnp.sum(jnp.where(lane == o, counts, 0.0), axis=1, keepdims=True).astype(jnp.int32)
    position = start + iota((cap, slab), 0)
    gather = jnp.concatenate(
        [one_hot(position == site) for site in shifted_sites(iota((cap, slab), 1), extent_x)], axis=0
    )
    slot_owner = iota((1, n_xyz * cap), 1) // cap
    slot_start = jnp.zeros((1, n_xyz * cap), jnp.int32)
    slot_count = jnp.zeros((1, n_xyz * cap), jnp.int32)
    for p in range(n_xyz):
        value = cnt[0, 0:1, p:p + 1]
        slot_start = slot_start + jnp.where(slot_owner > p, value, 0)
        slot_count = slot_count + jnp.where(slot_owner == p, value, 0)
    slot = iota((1, n_xyz * cap), 1) - slot_owner * cap
    slot_site = jnp.where(slot < slot_count, slot_start + slot, -1)
    held = one_hot(iota((slab, n_xyz * cap), 0) == slot_site)
    gather_tiles = dot(gather, held).astype(BF16)
    slot_lane = iota((slab, cap), 1)
    spread = one_hot((iota((slab, cap), 0) == start + slot_lane) & (slot_lane < own_count))

    load.wait()
    lane_q = iota((cap, LANES), 1)

    def minus_identity(q):
        place = lane_q + q * LANES
        return jnp.where((place >> 5) == (place & 31), -1.0, 0.0).astype(BF16)

    for group in range(3):
        rows = []
        for q in range(16):
            part_q = slice(q * LANES, (q + 1) * LANES)
            if group == 0:
                pieces = [links[m, :, part_q] for m in (0, 1, 2, 3)]
            elif group == 1:
                pieces = [links[m, :, part_q] for m in (4, 5, 6)] + [minus_identity(q)]
            else:
                pieces = [links[m, :, part_q] for m in (7, 8)]
            rows.append(jnp.concatenate(pieces, axis=1))
        stacked = jnp.concatenate(rows, axis=0)
        moved = dot(stacked, perm[0:stacked.shape[1], :]).astype(BF16)
        for q in range(16):
            for a in range(4):
                for g in range(2):
                    at = (q * 4 + a) * GROUP
                    first = q * cap + g * GROUP
                    weights[g, at:at + GROUP, group * LANES:(group + 1) * LANES] = moved[
                        first:first + GROUP, a * LANES:(a + 1) * LANES]

    def set_lhs(group, blocks):
        stacked = jnp.concatenate(
            [jnp.concatenate([b[:, u * LANES:(u + 1) * LANES] for b in blocks], axis=1) for u in range(UNITS)],
            axis=0,
        )
        moved = dot(stacked, perm[0:stacked.shape[1], :]).astype(BF16)
        for u in range(UNITS):
            for b in range(4):
                for g in range(2):
                    at = (u * 4 + b) * GROUP
                    first = u * cap + g * GROUP
                    lhs[g, at:at + GROUP, group * LANES:(group + 1) * LANES] = moved[
                        first:first + GROUP, b * LANES:(b + 1) * LANES]

    for copy in copies_n:
        copy.wait()
    away = []
    for side in range(2):
        row_start = start_of(cnt[1 + side, 0:1, :].astype(F32))
        away.append(one_hot(row_start + iota((cap, slab), 0) == iota((cap, slab), 1)))
    away = jnp.concatenate(away, axis=0)
    away_tiles = dot(away, held).astype(BF16)

    rhs_rows = None
    diagonal = (iota((GROUP, 512), 1) & (GROUP - 1)) == iota((GROUP, 512), 0)
    for sweep in range(SWEEPS):
        if sweep == 0:
            for copy in copies_a:
                copy.wait()
            source, near, far = vec, gather, away
        else:
            for copy in copies_c:
                copy.wait()
            source, near, far = tiles, gather_tiles, away_tiles
        full = source[...]
        zout[sweep] = dot(far, full).astype(BF16)
        copies_z = [
            remote(
                zout.at[sweep, pl.ds(side * cap, cap)], zin.at[sweep, pl.ds((1 - side) * cap, cap)],
                send_z.at[sweep, side], recv_z.at[sweep, side], (row, o),
            )
            for side, row in enumerate((up, down))
        ]
        around = dot(near, full).astype(BF16)
        blocks = [around[m * cap:(m + 1) * cap] for m in range(7)]
        if sweep == 0:
            rhs_rows = blocks[0]
        set_lhs(0, blocks[0:4])
        set_lhs(1, blocks[4:7] + [rhs_rows])
        for g in range(2):
            part[g] = dot_nt(lhs[g, :, 0:256], weights[g, :, 0:256])
        for copy in copies_z:
            copy.wait()
        set_lhs(2, [zin[sweep, 0:cap], zin[sweep, cap:2 * cap]])
        updated = []
        for g in range(2):
            total = part[g] + dot_nt(lhs[g, :, 256:384], weights[g, :, 256:384])
            rows = []
            for u in range(UNITS):
                pieces = []
                for r in range(2):
                    at = (u * 4 + r * 2) * GROUP
                    from_real, from_imag = total[at:at + GROUP], total[at + GROUP:at + 2 * GROUP]
                    real = from_imag[:, 512:] - from_real[:, :512]
                    imag = -(from_real[:, 512:] + from_imag[:, :512])
                    pieces += [jnp.where(diagonal, v, 0.0).astype(BF16) for v in (real, imag)]
                rows.append(jnp.concatenate(pieces, axis=1))
            picked = dot(jnp.concatenate(rows, axis=0), pick[...]).astype(BF16)
            updated.append(jnp.concatenate([picked[u * GROUP:(u + 1) * GROUP] for u in range(UNITS)], axis=1))
        tile = jnp.concatenate(updated, axis=0)
        if sweep < SWEEPS - 1:
            tiles[my_tile, :] = tile
            copies_c = to_slice(lambda peer: tiles.at[my_tile], tiles.at[my_tile], send_c, recv_c)
    scat[...] = dot(spread, tile).astype(BF16)
    copies_e = to_slice(
        lambda peer: scat.at[pl.ds(pl.multiple_of(peer * block, block), block)], fin.at[o], send_e, recv_e
    )
    fin[o] = scat[mine, :]
    for copy in copies_e:
        copy.wait()
    total = fin[0].astype(F32)
    for p in range(1, n_xyz):
        total = total + fin[p].astype(F32)
    own_ref[...] = total.astype(BF16)


def on_device(n_ta, n_xyz, residual, iterate, prolongator, coarse_links, owner_counts):
    block = residual.shape[0]
    cap = coarse_links.shape[1]
    slab = n_xyz * block
    basis_real = basis_block(prolongator)
    coarse_rhs = restrict(residual, basis_real)
    vmem = pl.BlockSpec(memory_space=pltpu.VMEM)
    dma = pltpu.SemaphoreType.DMA
    own_piece = pl.pallas_call(
        functools.partial(coarse_kernel, n_ta, n_xyz, cap, block),
        out_shape=jax.ShapeDtypeStruct((block, COLS), BF16),
        in_specs=[vmem, vmem, pl.BlockSpec(memory_space=pl.ANY)],
        out_specs=vmem,
        scratch_shapes=[
            pltpu.VMEM((slab, COLS), BF16),
            pltpu.VMEM((n_xyz * cap, COLS), BF16),
            pltpu.VMEM((n_xyz, block, COLS), BF16),
            pltpu.VMEM((slab, COLS), BF16),
            pltpu.VMEM((SWEEPS, 2 * cap, COLS), BF16),
            pltpu.VMEM((SWEEPS, 2 * cap, COLS), BF16),
            pltpu.VMEM((3, 8, LANES), jnp.int32),
            pltpu.VMEM(coarse_links.shape, BF16),
            pltpu.VMEM((2, 64 * GROUP, 3 * LANES), BF16),
            pltpu.VMEM((2, 24 * GROUP, 3 * LANES), BF16),
            pltpu.VMEM((2, 24 * GROUP, 64 * GROUP), F32),
            pltpu.VMEM((512, 512), BF16),
            pltpu.VMEM((2048, LANES), BF16),
            dma((n_xyz - 1,)), dma((n_xyz - 1,)),
            dma((n_xyz - 1,)), dma((n_xyz - 1,)),
            dma((n_xyz - 1,)), dma((n_xyz - 1,)),
            dma((SWEEPS, 2)), dma((SWEEPS, 2)),
            dma((2,)), dma((2,)),
            dma,
        ],
        compiler_params=pltpu.CompilerParams(
            collective_id=0, has_side_effects=True, vmem_limit_bytes=48 * 1024 * 1024
        ),
    )(coarse_rhs, owner_counts, coarse_links)
    correction = prolong(own_piece, basis_real)
    return (iterate.astype(F32) + correction).astype(BF16)


def solution(mesh):
    in_specs = (
        P(("ta", "xyz"), None),
        P(("ta", "xyz"), None),
        P(("ta", "xyz"), None),
        P(None, ("ta", "xyz"), None),
        P("ta", None),
    )
    out_specs = P(("ta", "xyz"), None)
    return jax.shard_map(
        functools.partial(on_device, mesh.shape["ta"], mesh.shape["xyz"]),
        mesh=mesh, in_specs=in_specs, out_specs=out_specs, check_vma=False,
    )
```

time: 115 us -> 36.8 us (0.32)
  local copies, waits for them, and re-layouts: 52.4 us -> 3.29 us
  Pallas kernels: 0 us -> 31.8 us
  blocking collectives: 29 us -> 0 us
  matrix products: 12.9 us -> 0.8 us
  other arithmetic: 12.1 us -> 0.71 us
  starting transfers between devices: 7.43 us -> 0 us
    pallas_call x0 -> x1, Pallas kernels: none -> 31.8 us  [on_device(): pl.pallas_call(functools.partial(coarse_kernel, n_ta, n_xyz, cap, block),...]
    all_gather x3 -> x0, blocking collectives: 29 us -> none  [the longest x2 18.3 us: on_device(): lax.all_gather(owned_tile, 'xyz', axis=0, tiled=True)]
    gather x20 -> x0, local copies, waits for them, and re-layouts: 17.5 us -> none  [the longest x12 8.9 us: on_device(): jnp.take(here_rows, rows, axis=0)]
    dot_general x4 -> x2, matrix products: 12.9 us -> 0.8 us  [the longest x1 0.45 us: restrict(): jnp.einsum('bkf,brf->brk', block, vector, preferred_element_type=F32)]
    unnamed x93 -> x9, local copies, waits for them, and re-layouts: 12.2 us -> 1.24 us
    ppermute x4 -> x0, starting transfers between devices: 7.43 us -> none  [the longest x2 7.42 us: with_halo(): lax.ppermute(lax.slice_in_dim(block, 0, width, axis=dim), axis, backward)]
    another operation x20 -> x0, local copies, waits for them, and re-layouts: 7.28 us -> none  [on_device(): neighbours = jnp.stack(row_list)]
    select_n x20 -> x0, other arithmetic: 6.38 us -> none  [the longest x15 3.76 us: on_device(): jnp.take(here_rows, rows, axis=0)]
  transfers between devices with their start and end apart: 4 -> 0, of which waited for: 0 -> 0; matrix products, arithmetic and copies ran while one was open for 33% -> 0% of each run, Pallas kernels for 0% -> 0%
where the time goes in v1:
time: 36.8 us; the launch traced here: 36.6 us
  Pallas kernels  31.8 us (86%)
  local copies, waits for them, and re-layouts  3.29 us (9%)
  matrix products  0.8 us (2%)
  other arithmetic  0.71 us (2%)
    pallas_call x1, Pallas kernels, on_device(): pl.pallas_call(functools.partial(coarse_kernel, n_ta, n_xyz, cap, block),...  31.8 us
    reshape x1, local copies, waits for them, and re-layouts, basis_block(): matrix = basis_rows.reshape(count_rows, 2, NV, FB)  1.66 us
    unnamed x9, local copies, waits for them, and re-layouts  1.24 us

profile of v1, /device:TPU:0, one launch (start us, length us, event | category | flops | bytes accessed | tf_op | source)
XLA Modules:
  0.0 36.6 jit_solution(2039297408257092763)
XLA Ops:
  0.0 0.0 copy-start.2
  0.0 1.7 %reshape.14 = bf16[16,2,32,192]{3,2,1,0:T(8,128)(2,1)S(1)} reshape(bf16[16,12288]{1,0:T(8,128)(2,1)} %param.7) | data formatting | bytes 786432 | tf_op jit(solution)/shard_map/reshape | solution.py:27
  1.7 0.0 copy-done.2
  1.8 0.1 reshape.15
  1.9 0.0 copy-start
  1.9 0.0 copy-start.1
  1.9 0.5 %fusion = bf16[16,12,64]{2,1,0:T(8,128)(2,1)S(1)} fusion(bf16[16,12,384]{2,1,0:T(8,128)(2,1)S(1)} %reshape.15, bf16[16,32,192]{2,1,0:T(8,128)(2,1)S(1)} %get-tuple-element.6, bf16[16,32,192]{2,1,0:T(8,128)(2,1)S(1)} %fusion.4, bf16[16,32,192]{2,1,0:T(8,128)(2,1)S(1)} %get-tuple-element.5), kind=kOutput, calls=%fused_computation.1 | convolution fusion | flops 12595200 | bytes 761856 | tf_op jit(solution)/shard_map/bkf,brf->brk/dot_general | solution.py:36
  2.4 0.1 convert_element_type.16.rhs_ref
  2.5 0.7 %copy-done = bf16[9,32,2048]{2,1,0:T(8,128)(2,1)S(1)} copy-done((bf16[9,32,2048]{2,1,0:T(8,128)(2,1)S(1)}, bf16[9,32,2048]{2,1,0:T(8,128)(2,1)}, u32[]{:S(2)}) %copy-start) | copy-done | bytes 1179672
  3.1 0.0 copy-done.1
  3.2 31.8 %shard_map.55 = bf16[16,768]{1,0:T(8,128)(2,1)S(1)} custom-call(bf16[16,768]{1,0:T(8,128)(2,1)S(1)} %convert_element_type.16.rhs_ref, s32[1,8]{1,0:T(1,128)S(1)} %copy-done.1, bf16[9,32,2048]{2,1,0:T(8,128)(2,1)S(1)} %copy-done), custom_call_target="tpu_custom_call" | custom-call | tf_op jit(solution)/shard_map/pallas_call | solution.py:284
  34.9 0.1 reshape.16
  35.0 0.0 copy-start.3
  35.0 0.3 fusion.1
  35.4 0.1 copy.10
  35.5 0.5 %copy-done.3 = bf16[16,4608]{1,0:T(8,128)(2,1)S(1)} copy-done((bf16[16,4608]{1,0:T(8,128)(2,1)S(1)}, bf16[16,4608]{1,0:T(8,128)(2,1)}, u32[]{:S(2)}) %copy-start.3) | copy-done | bytes 147480
  36.0 0.7 %add_convert_fusion = bf16[16,4608]{1,0:T(8,128)(2,1)} fusion(f32[16,4608]{1,0:T(8,128)S(1)} %bitcast.16, bf16[16,4608]{1,0:T(8,128)(2,1)S(1)} %copy-done.3), kind=kLoop, calls=%fused_computation.3 | loop fusion | flops 221184 | bytes 589824 | tf_op jit(solution)/shard_map/convert_element_type | solution.py:315
  (2 shorter events, 0.1 us)
Async XLA Ops:
  0.0 1.7 %copy-start.2 = (bf16[16,4608]{1,0:T(8,128)(2,1)S(1)}, bf16[16,4608]{1,0:T(8,128)(2,1)}, u32[]{:S(2)}) copy-start(bf16[16,4608]{1,0:T(8,128)(2,1)} %param.5) | copy-start | bytes 442372
  1.9 1.3 %copy-start = (bf16[9,32,2048]{2,1,0:T(8,128)(2,1)S(1)}, bf16[9,32,2048]{2,1,0:T(8,128)(2,1)}, u32[]{:S(2)}) copy-start(bf16[9,32,2048]{2,1,0:T(8,128)(2,1)} %links_hbm.1) | copy-start | bytes 3538948
  1.9 1.3 %copy-start.1 = (s32[1,8]{1,0:T(1,128)S(1)}, s32[1,8]{1,0:T(1,128)}, u32[]{:S(2)}) copy-start(s32[1,8]{1,0:T(1,128)} %counts_ref.1) | copy-start | bytes 100
  35.0 0.9 %copy-start.3 = (bf16[16,4608]{1,0:T(8,128)(2,1)S(1)}, bf16[16,4608]{1,0:T(8,128)(2,1)}, u32[]{:S(2)}) copy-start(bf16[16,4608]{1,0:T(8,128)(2,1)} %param.6) | copy-start | bytes 442372

commit v2 on v1

--- a/solution.py
+++ b/solution.py
@@ -83,8 +83,8 @@
 def coarse_kernel(
     n_ta, n_xyz, cap, block,
     rhs_ref, counts_ref, links_hbm, own_ref,
-    vec, tiles, fin, scat, zin, zout, cnt, links, weights, lhs, part, perm, pick,
-    send_a, recv_a, send_c, recv_c, send_e, recv_e, send_z, recv_z, send_n, recv_n, sem_l,
+    vec, tiles, fin, scat, zin, zout, beside, cnt, links, weights, lhs, part, perm, pick,
+    send_a, recv_a, send_c, recv_c, send_e, recv_e, send_z, recv_z, send_b, recv_b, send_n, recv_n, sem_l,
 ):
     slab = n_xyz * block
     extent_x = slab // (LY * LZ)
@@ -100,14 +100,15 @@
     for peer in peers:
         pl.semaphore_signal(barrier, inc=1, device_id=(t, peer), device_id_type=MESH)
     for row in (up, down):
-        pl.semaphore_signal(barrier, inc=1, device_id=(row, o), device_id_type=MESH)
+        for peer in [o] + peers:
+            pl.semaphore_signal(barrier, inc=1, device_id=(row, peer), device_id_type=MESH)
 
     cnt[0] = jnp.zeros((8, LANES), jnp.int32)
     cnt[0, 0:1, 0:n_xyz] = counts_ref[...]
     mine = pl.ds(pl.multiple_of(o * block, block), block)
     my_tile = pl.ds(pl.multiple_of(o * cap, cap), cap)
     vec[mine, :] = rhs_ref[...]
-    pl.semaphore_wait(barrier, n_xyz + 1)
+    pl.semaphore_wait(barrier, 3 * n_xyz - 1)
 
     def remote(src, dst, send, recv, device):
         copy = pltpu.make_async_remote_copy(
@@ -128,6 +129,11 @@
         for side, row in enumerate((down, up))
     ]
     copies_a = to_slice(lambda peer: vec.at[mine], vec.at[mine], send_a, recv_a)
+    copies_b = [
+        remote(vec.at[mine], beside.at[1 - side, mine], send_b.at[side, d], recv_b.at[side, d], (row, peer))
+        for d, peer in enumerate([o] + peers)
+        for side, row in enumerate((up, down))
+    ]
 
     r_id, c_id = iota((512, 512), 0), iota((512, 512), 1)
     perm[...] = one_hot(c_id == ((r_id >> 5) & 3) * 128 + (r_id >> 7) * 32 + (r_id & 31))
@@ -201,35 +207,27 @@
                     lhs[g, at:at + GROUP, group * LANES:(group + 1) * LANES] = moved[
                         first:first + GROUP, b * LANES:(b + 1) * LANES]
 
-    for copy in copies_n:
-        copy.wait()
-    away = []
-    for side in range(2):
-        row_start = start_of(cnt[1 + side, 0:1, :].astype(F32))
-        away.append(one_hot(row_start + iota((cap, slab), 0) == iota((cap, slab), 1)))
-    away = jnp.concatenate(away, axis=0)
-    away_tiles = dot(away, held).astype(BF16)
-
     rhs_rows = None
     diagonal = (iota((GROUP, 512), 1) & (GROUP - 1)) == iota((GROUP, 512), 0)
     for sweep in range(SWEEPS):
         if sweep == 0:
             for copy in copies_a:
                 copy.wait()
-            source, near, far = vec, gather, away
+            source, near = vec, gather
         else:
             for copy in copies_c:
                 copy.wait()
-            source, near, far = tiles, gather_tiles, away_tiles
+            source, near = tiles, gather_tiles
         full = source[...]
-        zout[sweep] = dot(far, full).astype(BF16)
-        copies_z = [
-            remote(
-                zout.at[sweep, pl.ds(side * cap, cap)], zin.at[sweep, pl.ds((1 - side) * cap, cap)],
-                send_z.at[sweep, side], recv_z.at[sweep, side], (row, o),
-            )
-            for side, row in enumerate((up, down))
-        ]
+        if sweep > 0:
+            zout[...] = dot(away_tiles, full).astype(BF16)
+            copies_z = [
+                remote(
+                    zout.at[pl.ds(side * cap, cap)], zin.at[pl.ds((1 - side) * cap, cap)],
+                    send_z.at[side], recv_z.at[side], (row, o),
+                )
+                for side, row in enumerate((up, down))
+            ]
         around = dot(near, full).astype(BF16)
         blocks = [around[m * cap:(m + 1) * cap] for m in range(7)]
         if sweep == 0:
@@ -238,9 +236,14 @@
         set_lhs(1, blocks[4:7] + [rhs_rows])
         for g in range(2):
             part[g] = dot_nt(lhs[g, :, 0:256], weights[g, :, 0:256])
-        for copy in copies_z:
-            copy.wait()
-        set_lhs(2, [zin[sweep, 0:cap], zin[sweep, cap:2 * cap]])
+        if sweep == 0:
+            for copy in copies_b:
+                copy.wait()
+            set_lhs(2, [dot(gather[0:cap], beside[side]).astype(BF16) for side in range(2)])
+        else:
+            for copy in copies_z:
+                copy.wait()
+            set_lhs(2, [zin[0:cap], zin[cap:2 * cap]])
         updated = []
         for g in range(2):
             total = part[g] + dot_nt(lhs[g, :, 256:384], weights[g, :, 256:384])
@@ -260,6 +263,14 @@
         if sweep < SWEEPS - 1:
             tiles[my_tile, :] = tile
             copies_c = to_slice(lambda peer: tiles.at[my_tile], tiles.at[my_tile], send_c, recv_c)
+            for copy in copies_n:
+                copy.wait()
+            away = []
+            for side in range(2):
+                row_start = start_of(cnt[1 + side, 0:1, :].astype(F32))
+                away.append(one_hot(row_start + iota((cap, slab), 0) == iota((cap, slab), 1)))
+            away = jnp.concatenate(away, axis=0)
+            away_tiles = dot(away, held).astype(BF16)
     scat[...] = dot(spread, tile).astype(BF16)
     copies_e = to_slice(
         lambda peer: scat.at[pl.ds(pl.multiple_of(peer * block, block), block)], fin.at[o], send_e, recv_e
@@ -291,8 +302,9 @@
             pltpu.VMEM((n_xyz * cap, COLS), BF16),
             pltpu.VMEM((n_xyz, block, COLS), BF16),
             pltpu.VMEM((slab, COLS), BF16),
-            pltpu.VMEM((SWEEPS, 2 * cap, COLS), BF16),
-            pltpu.VMEM((SWEEPS, 2 * cap, COLS), BF16),
+            pltpu.VMEM((2 * cap, COLS), BF16),
+            pltpu.VMEM((2 * cap, COLS), BF16),
+            pltpu.VMEM((2, slab, COLS), BF16),
             pltpu.VMEM((3, 8, LANES), jnp.int32),
             pltpu.VMEM(coarse_links.shape, BF16),
             pltpu.VMEM((2, 64 * GROUP, 3 * LANES), BF16),
@@ -303,12 +315,13 @@
             dma((n_xyz - 1,)), dma((n_xyz - 1,)),
             dma((n_xyz - 1,)), dma((n_xyz - 1,)),
             dma((n_xyz - 1,)), dma((n_xyz - 1,)),
-            dma((SWEEPS, 2)), dma((SWEEPS, 2)),
+            dma((2,)), dma((2,)),
+            dma((2, n_xyz)), dma((2, n_xyz)),
             dma((2,)), dma((2,)),
             dma,
         ],
         compiler_params=pltpu.CompilerParams(
-            collective_id=0, has_side_effects=True, vmem_limit_bytes=48 * 1024 * 1024
+            collective_id=0, has_side_effects=True, vmem_limit_bytes=60 * 1024 * 1024
         ),
     )(coarse_rhs, owner_counts, coarse_links)
     correction = prolong(own_piece, basis_real)

time: 36.8 us -> 43.6 us (1.18)
  Pallas kernels: 31.8 us -> 37.8 us
  local copies, waits for them, and re-layouts: 3.29 us -> 3.95 us
    pallas_call x1, Pallas kernels: 31.8 us -> 37.8 us  [on_device(): pl.pallas_call(functools.partial(coarse_kernel, n_ta, n_xyz, cap, block),...]
    reshape x1, local copies, waits for them, and re-layouts: 0.11 us -> 0.85 us  [prolong(): vector = coarse_rows.reshape(count_rows, RHS, 2 * NV)]
    unnamed x9 -> x5, local copies, waits for them, and re-layouts: 1.24 us -> 0.56 us
    convert_element_type x1, local copies, waits for them, and re-layouts: 0.12 us -> 0.73 us  [restrict(): return result.reshape(count_rows, COLS).astype(BF16)]
where the time goes in v2:
time: 43.6 us; the launch traced here: 43.3 us
  Pallas kernels  37.8 us (87%)
  local copies, waits for them, and re-layouts  3.95 us (9%)
  matrix products  0.8 us (2%)
  other arithmetic  0.71 us (2%)
    pallas_call x1, Pallas kernels, on_device(): pl.pallas_call(functools.partial(coarse_kernel, n_ta, n_xyz, cap, block),...  37.8 us
    reshape x1, local copies, waits for them, and re-layouts, basis_block(): matrix = basis_rows.reshape(count_rows, 2, NV, FB)  1.66 us

profile of v2, /device:TPU:0, one launch (start us, length us, event | category | flops | bytes accessed | tf_op | source)
XLA Modules:
  0.0 43.3 jit_solution(6030932825383595877)
XLA Ops:
  0.0 0.0 copy-start
  0.0 1.7 %reshape.14 = bf16[16,2,32,192]{3,2,1,0:T(8,128)(2,1)S(1)} reshape(bf16[16,12288]{1,0:T(8,128)(2,1)} %param.7) | data formatting | bytes 786432 | tf_op jit(solution)/shard_map/reshape | solution.py:27
  1.7 0.0 copy-done
  1.8 0.1 reshape.15
  1.9 0.5 %fusion = bf16[16,12,64]{2,1,0:T(8,128)(2,1)S(1)} fusion(bf16[16,12,384]{2,1,0:T(8,128)(2,1)S(1)} %reshape.15, bf16[16,32,192]{2,1,0:T(8,128)(2,1)S(1)} %get-tuple-element.6, bf16[16,32,192]{2,1,0:T(8,128)(2,1)S(1)} %fusion.4, bf16[16,32,192]{2,1,0:T(8,128)(2,1)S(1)} %get-tuple-element.5), kind=kOutput, calls=%fused_computation.1 | convolution fusion | flops 12595200 | bytes 761856 | tf_op jit(solution)/shard_map/bkf,brf->brk/dot_general | solution.py:36
  2.3 0.7 %convert_element_type.16.rhs_ref = bf16[16,768]{1,0:T(8,128)(2,1)} reshape(bf16[16,12,64]{2,1,0:T(8,128)(2,1)S(1)} %fusion) | data formatting | bytes 49152 | tf_op jit(solution)/shard_map/convert_element_type | solution.py:37
  3.1 37.8 %shard_map.55 = bf16[16,768]{1,0:T(8,128)(2,1)} custom-call(bf16[16,768]{1,0:T(8,128)(2,1)} %convert_element_type.16.rhs_ref, s32[1,8]{1,0:T(1,128)} %counts_ref.1, bf16[9,32,2048]{2,1,0:T(8,128)(2,1)} %links_hbm.1), custom_call_target="tpu_custom_call" | custom-call | tf_op jit(solution)/shard_map/pallas_call | solution.py:295
  40.8 0.8 %reshape.16 = bf16[16,12,64]{2,1,0:T(8,128)(2,1)S(1)} reshape(bf16[16,768]{1,0:T(8,128)(2,1)} %shard_map.55) | data formatting | bytes 49152 | tf_op jit(solution)/shard_map/reshape | solution.py:42
  41.7 0.0 copy-start.1
  41.7 0.3 fusion.1
  42.0 0.1 copy.10
  42.1 0.5 %copy-done.1 = bf16[16,4608]{1,0:T(8,128)(2,1)S(1)} copy-done((bf16[16,4608]{1,0:T(8,128)(2,1)S(1)}, bf16[16,4608]{1,0:T(8,128)(2,1)}, u32[]{:S(2)}) %copy-start.1) | copy-done | bytes 147480
  42.6 0.7 %add_convert_fusion = bf16[16,4608]{1,0:T(8,128)(2,1)} fusion(f32[16,4608]{1,0:T(8,128)S(1)} %bitcast.16, bf16[16,4608]{1,0:T(8,128)(2,1)S(1)} %copy-done.1), kind=kLoop, calls=%fused_computation.3 | loop fusion | flops 221184 | bytes 589824 | tf_op jit(solution)/shard_map/convert_element_type | solution.py:328
  (2 shorter events, 0.1 us)
Async XLA Ops:
  0.0 1.7 %copy-start = (bf16[16,4608]{1,0:T(8,128)(2,1)S(1)}, bf16[16,4608]{1,0:T(8,128)(2,1)}, u32[]{:S(2)}) copy-start(bf16[16,4608]{1,0:T(8,128)(2,1)} %param.5) | copy-start | bytes 442372
  41.7 0.9 %copy-start.1 = (bf16[16,4608]{1,0:T(8,128)(2,1)S(1)}, bf16[16,4608]{1,0:T(8,128)(2,1)}, u32[]{:S(2)}) copy-start(bf16[16,4608]{1,0:T(8,128)(2,1)} %param.6) | copy-start | bytes 442372

commit v3 on v1

--- a/solution.py
+++ b/solution.py
@@ -22,28 +22,6 @@
 BF16 = jnp.bfloat16
 
 
-def basis_block(basis_rows):
-    count_rows = basis_rows.shape[0]
-    matrix = basis_rows.reshape(count_rows, 2, NV, FB)
-    real_rows = jnp.concatenate([matrix[:, 0], matrix[:, 1]], axis=2)
-    imag_rows = jnp.concatenate([-matrix[:, 1], matrix[:, 0]], axis=2)
-    return jnp.concatenate([real_rows, imag_rows], axis=1)
-
-
-def restrict(fine_rows, block):
-    count_rows = fine_rows.shape[0]
-    vector = fine_rows.reshape(count_rows, RHS, 2 * FB)
-    result = jnp.einsum("bkf,brf->brk", block, vector, preferred_element_type=F32)
-    return result.reshape(count_rows, COLS).astype(BF16)
-
-
-def prolong(coarse_rows, block):
-    count_rows = coarse_rows.shape[0]
-    vector = coarse_rows.reshape(count_rows, RHS, 2 * NV)
-    result = jnp.einsum("bkf,brk->brf", block, vector, preferred_element_type=F32)
-    return result.reshape(count_rows, RHS * 2 * FB)
-
-
 def iota(shape, dim):
     return lax.broadcasted_iota(jnp.int32, shape, dim)
 
@@ -80,11 +58,79 @@
     ]
 
 
+def on_diagonal(shape):
+    return (iota(shape, 1) & (GROUP - 1)) == (iota(shape, 0) & (GROUP - 1))
+
+
+def restrict(residual, basis, basis_rows, spots):
+    wide = 2 * LANES
+    lane = iota((GROUP, wide), 1)
+    for h in range(2):
+        for pair in range(NV):
+            first = pair * 2 * FB + h * LANES
+            basis_rows[h, pair * GROUP:(pair + 1) * GROUP, :] = basis[:, first:first + wide]
+    real, imag = [], []
+    for r in range(RHS):
+        first = r * 2 * FB
+        real.append(jnp.where(lane < FB, residual[:, first:first + wide], 0.0).astype(BF16))
+        imag.append(jnp.where(lane >= wide - FB, residual[:, first + LANES:first + LANES + wide], 0.0).astype(BF16))
+    real, imag = jnp.concatenate(real, axis=0), jnp.concatenate(imag, axis=0)
+    row_id, col_id = iota((wide, wide), 0), iota((wide, wide), 1)
+    real_late = dot(real, one_hot(col_id == row_id + 64)).astype(BF16)
+    imag_early = dot(imag, one_hot(col_id == row_id - 64)).astype(BF16)
+    lines = RHS * GROUP
+    keep = on_diagonal((lines, wide))
+    pieces = {}
+    for h, pair in enumerate(((real, imag_early), (real_late, imag))):
+        x = dot_nt(jnp.concatenate(pair, axis=0), basis_rows[h])
+        re = x[:lines, :wide] + x[lines:, wide:]
+        im = x[lines:, :wide] - x[:lines, wide:]
+        pieces[0, h] = jnp.where(keep, re, 0.0).astype(BF16)
+        pieces[1, h] = jnp.where(keep, im, 0.0).astype(BF16)
+    rows = []
+    for u in range(UNITS):
+        line = [
+            pieces[c, h][(2 * u + r) * GROUP:(2 * u + r + 1) * GROUP]
+            for r in range(2) for c in range(2) for h in range(2)
+        ]
+        rows.append(jnp.concatenate(line, axis=1))
+    picked = dot(jnp.concatenate(rows, axis=0), spots[...]).astype(BF16)
+    return jnp.concatenate([picked[u * GROUP:(u + 1) * GROUP] for u in range(UNITS)], axis=1)
+
+
+def prolong(coarse, basis_rows, spots, iterate, out_ref):
+    wide = 2 * LANES
+    stacked = jnp.concatenate([coarse[:, u * LANES:(u + 1) * LANES] for u in range(UNITS)], axis=0)
+    spread = dot_nt(stacked, spots[...])
+    spread = jnp.where(on_diagonal(spread.shape), spread, 0.0).astype(BF16)
+    moved = []
+    for h in range(2):
+        upper, lower = [], []
+        for r in range(RHS):
+            u = r // 2
+            first = (r % 2) * 1024 + h * wide
+            re = spread[u * GROUP:(u + 1) * GROUP, first:first + wide]
+            im = spread[u * GROUP:(u + 1) * GROUP, first + 512:first + 512 + wide]
+            upper.append(jnp.concatenate([re, -im], axis=1))
+            lower.append(jnp.concatenate([im, re], axis=1))
+        moved.append(dot(jnp.concatenate(upper + lower, axis=0), basis_rows[h]))
+    lines = RHS * GROUP
+    real = moved[0][:lines] + pltpu.roll(moved[1][:lines], wide - 64, 1)
+    imag = moved[1][lines:] + pltpu.roll(moved[0][lines:], 64, 1)
+    low = iota((GROUP, LANES), 1) < 64
+    for r in range(RHS):
+        re, im = real[r * GROUP:(r + 1) * GROUP], imag[r * GROUP:(r + 1) * GROUP]
+        tiles = (re[:, :LANES], jnp.where(low, re[:, LANES:], im[:, :LANES]), im[:, LANES:])
+        for i, tile in enumerate(tiles):
+            part = slice((r * 3 + i) * LANES, (r * 3 + i + 1) * LANES)
+            out_ref[:, part] = (iterate[:, part].astype(F32) + tile).astype(BF16)
+
+
 def coarse_kernel(
     n_ta, n_xyz, cap, block,
-    rhs_ref, counts_ref, links_hbm, own_ref,
-    vec, tiles, fin, scat, zin, zout, cnt, links, weights, lhs, part, perm, pick,
-    send_a, recv_a, send_c, recv_c, send_e, recv_e, send_z, recv_z, send_n, recv_n, sem_l,
+    residual_hbm, iterate_hbm, basis_hbm, counts_ref, links_hbm, out_ref,
+    residual, iterate, basis, basis_rows, spots, vec, tiles, fin, scat, zin, zout, cnt, links, weights, lhs, part, perm, pick,
+    send_a, recv_a, send_c, recv_c, send_e, recv_e, send_z, recv_z, send_n, recv_n, sem_l, sem_r, sem_i, sem_b,
 ):
     slab = n_xyz * block
     extent_x = slab // (LY * LZ)
@@ -94,8 +140,14 @@
     down = lax.rem(t + n_ta - 1, n_ta)
     peers = [lax.rem(o + d, n_xyz) for d in range(1, n_xyz)]
 
+    load_r = pltpu.make_async_copy(residual_hbm, residual, sem_r)
+    load_r.start()
+    load_b = pltpu.make_async_copy(basis_hbm, basis, sem_b)
+    load_b.start()
     load = pltpu.make_async_copy(links_hbm, links, sem_l)
     load.start()
+    load_i = pltpu.make_async_copy(iterate_hbm, iterate, sem_i)
+    load_i.start()
     barrier = pltpu.get_barrier_semaphore()
     for peer in peers:
         pl.semaphore_signal(barrier, inc=1, device_id=(t, peer), device_id_type=MESH)
@@ -106,7 +158,11 @@
     cnt[0, 0:1, 0:n_xyz] = counts_ref[...]
     mine = pl.ds(pl.multiple_of(o * block, block), block)
     my_tile = pl.ds(pl.multiple_of(o * cap, cap), cap)
-    vec[mine, :] = rhs_ref[...]
+    spot_id, spot_lane = iota((2048, LANES), 0), iota((2048, LANES), 1)
+    spots[...] = one_hot(spot_lane == (spot_id >> 9) * 32 + ((spot_id >> 4) & 15) * 2 + ((spot_id >> 8) & 1))
+    load_r.wait()
+    load_b.wait()
+    vec[mine, :] = restrict(residual, basis, basis_rows, spots)
     pl.semaphore_wait(barrier, n_xyz + 1)
 
     def remote(src, dst, send, recv, device):
@@ -270,23 +326,28 @@
     total = fin[0].astype(F32)
     for p in range(1, n_xyz):
         total = total + fin[p].astype(F32)
-    own_ref[...] = total.astype(BF16)
+    load_i.wait()
+    prolong(total.astype(BF16), basis_rows, spots, iterate, out_ref)
 
 
 def on_device(n_ta, n_xyz, residual, iterate, prolongator, coarse_links, owner_counts):
     block = residual.shape[0]
     cap = coarse_links.shape[1]
     slab = n_xyz * block
-    basis_real = basis_block(prolongator)
-    coarse_rhs = restrict(residual, basis_real)
     vmem = pl.BlockSpec(memory_space=pltpu.VMEM)
+    hbm = pl.BlockSpec(memory_space=pl.ANY)
     dma = pltpu.SemaphoreType.DMA
-    own_piece = pl.pallas_call(
+    return pl.pallas_call(
         functools.partial(coarse_kernel, n_ta, n_xyz, cap, block),
-        out_shape=jax.ShapeDtypeStruct((block, COLS), BF16),
-        in_specs=[vmem, vmem, pl.BlockSpec(memory_space=pl.ANY)],
+        out_shape=jax.ShapeDtypeStruct(residual.shape, BF16),
+        in_specs=[hbm, hbm, hbm, vmem, hbm],
         out_specs=vmem,
         scratch_shapes=[
+            pltpu.VMEM(residual.shape, BF16),
+            pltpu.VMEM(iterate.shape, BF16),
+            pltpu.VMEM(prolongator.shape, BF16),
+            pltpu.VMEM((2, NV * GROUP, 2 * LANES), BF16),
+            pltpu.VMEM((2048, LANES), BF16),
             pltpu.VMEM((slab, COLS), BF16),
             pltpu.VMEM((n_xyz * cap, COLS), BF16),
             pltpu.VMEM((n_xyz, block, COLS), BF16),
@@ -305,14 +366,12 @@
             dma((n_xyz - 1,)), dma((n_xyz - 1,)),
             dma((SWEEPS, 2)), dma((SWEEPS, 2)),
             dma((2,)), dma((2,)),
-            dma,
+            dma, dma, dma, dma,
         ],
         compiler_params=pltpu.CompilerParams(
-            collective_id=0, has_side_effects=True, vmem_limit_bytes=48 * 1024 * 1024
+            collective_id=0, has_side_effects=True, vmem_limit_bytes=60 * 1024 * 1024
         ),
-    )(coarse_rhs, owner_counts, coarse_links)
-    correction = prolong(own_piece, basis_real)
-    return (iterate.astype(F32) + correction).astype(BF16)
+    )(residual, iterate, prolongator, owner_counts, coarse_links)
 
 
 def solution(mesh):

time: 36.8 us -> 35.2 us (0.957)
  local copies, waits for them, and re-layouts: 3.29 us -> 1.58 us
  Pallas kernels: 31.8 us -> 33.5 us
  matrix products: 0.8 us -> 0 us
  other arithmetic: 0.71 us -> 0 us
    reshape x3 -> x0, local copies, waits for them, and re-layouts: 1.89 us -> none  [the longest x1 1.66 us: basis_block(): matrix = basis_rows.reshape(count_rows, 2, NV, FB)]
    pallas_call x1, Pallas kernels: 31.8 us -> 33.5 us  [on_device(): pl.pallas_call(functools.partial(coarse_kernel, n_ta, n_xyz, cap, block),...]
    dot_general x2 -> x0, matrix products: 0.8 us -> none  [the longest x1 0.45 us: restrict(): jnp.einsum('bkf,brf->brk', block, vector, preferred_element_type=F32)]
    convert_element_type x1 -> x0, other arithmetic: 0.69 us -> none  [on_device(): return (iterate.astype(F32) + correction).astype(BF16)]
    unnamed x9 -> x1, local copies, waits for them, and re-layouts: 1.24 us -> 1.58 us
where the time goes in v3:
time: 35.2 us; the launch traced here: 35.1 us
  Pallas kernels  33.5 us (95%)
  local copies, waits for them, and re-layouts  1.58 us (4%)
    pallas_call x1, Pallas kernels, on_device(): pl.pallas_call(functools.partial(coarse_kernel, n_ta, n_xyz, cap, block),...  33.5 us
    unnamed x1, local copies, waits for them, and re-layouts  1.58 us

profile of v3, /device:TPU:0, one launch (start us, length us, event | category | flops | bytes accessed | tf_op | source)
XLA Modules:
  0.0 35.1 jit_solution(4098325013341916482)
XLA Ops:
  0.0 33.5 %shard_map.55 = bf16[16,4608]{1,0:T(8,128)(2,1)} custom-call(bf16[16,4608]{1,0:T(8,128)(2,1)} %residual_hbm.1, bf16[16,4608]{1,0:T(8,128)(2,1)} %iterate_hbm.1, bf16[16,12288]{1,0:T(8,128)(2,1)} %basis_hbm.1, s32[1,8]{1,0:T(1,128)} %counts_ref.1, bf16[9,32,2048]{2,1,0:T(8,128)(2,1)} %links_hbm.1), custom_call_target="tpu_custom_call" | custom-call | tf_op jit(solution)/shard_map/pallas_call | solution.py:340
  33.5 1.6 %copy.7 = bf16[16,4608]{1,0:T(8,128)(2,1)} copy(bf16[16,4608]{1,0:T(8,128)(2,1)} %shard_map.55) | data formatting | bytes 294912

commit v4 on v3

--- a/solution.py
+++ b/solution.py
@@ -123,7 +123,7 @@
         tiles = (re[:, :LANES], jnp.where(low, re[:, LANES:], im[:, :LANES]), im[:, LANES:])
         for i, tile in enumerate(tiles):
             part = slice((r * 3 + i) * LANES, (r * 3 + i + 1) * LANES)
-            out_ref[:, part] = (iterate[:, part].astype(F32) + tile).astype(BF16)
+            out_ref[:, part] = iterate[:, part].astype(F32) + tile
 
 
 def coarse_kernel(
@@ -337,9 +337,9 @@
     vmem = pl.BlockSpec(memory_space=pltpu.VMEM)
     hbm = pl.BlockSpec(memory_space=pl.ANY)
     dma = pltpu.SemaphoreType.DMA
-    return pl.pallas_call(
+    summed = pl.pallas_call(
         functools.partial(coarse_kernel, n_ta, n_xyz, cap, block),
-        out_shape=jax.ShapeDtypeStruct(residual.shape, BF16),
+        out_shape=jax.ShapeDtypeStruct(residual.shape, F32),
         in_specs=[hbm, hbm, hbm, vmem, hbm],
         out_specs=vmem,
         scratch_shapes=[
@@ -372,6 +372,7 @@
             collective_id=0, has_side_effects=True, vmem_limit_bytes=60 * 1024 * 1024
         ),
     )(residual, iterate, prolongator, owner_counts, coarse_links)
+    return summed.astype(BF16)
 
 
 def solution(mesh):

time: 35.2 us -> 35.4 us (level)
  other arithmetic: 0 us -> 1.64 us
  local copies, waits for them, and re-layouts: 1.58 us -> 0 us
    convert_element_type x0 -> x1, other arithmetic: none -> 1.64 us  [on_device(): return summed.astype(BF16)]
    unnamed x1 -> x0, local copies, waits for them, and re-layouts: 1.58 us -> none
where the time goes in v4:
time: 35.4 us; the launch traced here: 35.2 us
  Pallas kernels  33.5 us (95%)
  other arithmetic  1.64 us (5%)
    pallas_call x1, Pallas kernels, on_device(): pl.pallas_call(functools.partial(coarse_kernel, n_ta, n_xyz, cap, block),...  33.5 us
    convert_element_type x1, other arithmetic, on_device(): return summed.astype(BF16)  1.64 us

profile of v4, /device:TPU:0, one launch (start us, length us, event | category | flops | bytes accessed | tf_op | source)
XLA Modules:
  0.0 35.2 jit_solution(7408946434726981699)
XLA Ops:
  0.0 33.5 %shard_map.55 = f32[16,4608]{1,0:T(8,128)} custom-call(bf16[16,4608]{1,0:T(8,128)(2,1)} %residual_hbm.1, bf16[16,4608]{1,0:T(8,128)(2,1)} %iterate_hbm.1, bf16[16,12288]{1,0:T(8,128)(2,1)} %basis_hbm.1, s32[1,8]{1,0:T(1,128)} %counts_ref.1, bf16[9,32,2048]{2,1,0:T(8,128)(2,1)} %links_hbm.1), custom_call_target="tpu_custom_call" | custom-call | tf_op jit(solution)/shard_map/pallas_call | solution.py:340
  33.5 1.6 %convert_element_type.3 = bf16[16,4608]{1,0:T(8,128)(2,1)} convert(f32[16,4608]{1,0:T(8,128)} %shard_map.55) | non-fusion elementwise | flops 73728 | bytes 442368 | tf_op jit(solution)/shard_map/convert_element_type | solution.py:375
